TPU v7x, 256 devices: a whole 4x4x8 slice. The times are simulated.
256 devices in a mesh: stn: 32 (over y, z), tm: 8 (over x, core).
Axes of the slice: x: 4, y: 4, z: 8, core: 2. Of those that a mesh axis runs over, the one named last changes fastest.
Arguments:
- voltages: bfloat16 [2, 512, 32, 16384], P(None, 'stn', None, 'tm'), may hold values from -6 to 6
- fir_taps: float32 [16, 64], replicated, may hold values from -1.5 to 1.5
Outputs:
- visibilities: bfloat16 [32, 64, 2, 512, 512], P('stn', 'tm')
All inputs are finite; a program needn't handle non-finite values.
Results may differ from a plain program's by a relative error of at most 0.0052.
Values may be sent and summed in bfloat16 or wider, within the bound.
A program may use at most 128 MiB of HBM per device.

v0:
```python
import math

import jax
import jax.numpy as jnp
from jax import lax
from jax.sharding import PartitionSpec as P


def shifted(block, axis, distance):
    devices = range(lax.axis_size(axis))
    route = [(i - distance, i) for i in devices if i - distance in devices]
    return lax.ppermute(block, axis, route)


def dft_tables(count):
    index = jnp.arange(count, dtype=jnp.int32)
    product = index[:, None] * index[None, :] % count
    angle = product.astype(jnp.float32) * (2.0 * math.pi / count)
    return (jnp.cos(angle), jnp.sin(angle))


def make_spectra(extended, fir_taps, spec_count):
    taps, branches = fir_taps.shape
    frames = extended.reshape(extended.shape[:-1] + (spec_count + taps - 1, branches)).astype(
        jnp.float32
    )
    filtered = jnp.zeros(frames.shape[:-2] + (spec_count, branches), jnp.float32)
    for tap_index in range(taps):
        begin = taps - 1 - tap_index
        filtered = filtered + fir_taps[tap_index] * frames[..., begin : begin + spec_count, :]
    cosine, sine_table = dft_tables(branches)
    high = lax.Precision.HIGHEST
    scale = 1.0 / math.sqrt(branches)
    real_in = filtered[0]
    imag_in = filtered[1]
    real_out = (
        jnp.einsum("...b,bk->...k", real_in, cosine, precision=high)
        + jnp.einsum("...b,bk->...k", imag_in, sine_table, precision=high)
    ) * scale
    imag_out = (
        jnp.einsum("...b,bk->...k", imag_in, cosine, precision=high)
        - jnp.einsum("...b,bk->...k", real_in, sine_table, precision=high)
    ) * scale
    stacked = jnp.stack([real_out, imag_out], 0)
    return jnp.transpose(stacked, (4, 3, 0, 2, 1)).astype(jnp.bfloat16)


def body(voltages, fir_taps):
    taps, branches = fir_taps.shape
    samples = voltages.shape[3]
    spec_count = samples // branches
    history_len = (taps - 1) * branches
    turned = lax.all_to_all(voltages, "stn", split_axis=2, concat_axis=1, tiled=True)
    history_part = shifted(turned[..., samples - history_len :], "tm", 1)
    extended = jnp.concatenate([history_part, turned], axis=3)
    local_spectra = make_spectra(extended, fir_taps, spec_count)
    gathered = lax.all_to_all(local_spectra, "tm", split_axis=0, concat_axis=1, tiled=True)
    channels, total_spec, _, _, inputs = gathered.shape
    matrix = gathered.reshape(channels, total_spec, 2 * inputs)
    gram = lax.dot_general(
        matrix, matrix, (((1,), (1,)), ((0,), (0,))), preferred_element_type=jnp.float32
    )
    vis_real = gram[:, :inputs, :inputs] + gram[:, inputs:, inputs:]
    vis_imag = gram[:, inputs:, :inputs] - gram[:, :inputs, inputs:]
    result = jnp.stack([vis_real, vis_imag], 1) * (1.0 / total_spec)
    return result[None].astype(jnp.bfloat16)


def solution(mesh):
    placed = (P(None, "stn", None, "tm"), P())
    return jax.shard_map(
        body,
        mesh=mesh,
        in_specs=placed,
        out_specs=P("stn", "tm", None, None, None),
        check_vma=False,
    )
```

profile of v0, /device:TPU:32, one launch (start us, length us, event | category | flops | bytes accessed | tf_op | source)
XLA Modules:
  0.0 315.0 jit_solution(10210632768420136778)
XLA Ops:
  0.0 4.5 %copy.20 = bf16[2,16,32,2048]{3,1,0,2:T(8,128)(2,1)S(1)} copy(bf16[2,16,32,2048]{3,2,1,0:T(8,128)(2,1)} %param.2) | data formatting | bytes 8388608 | tf_op args[0]
  4.5 107.1 %all_to_all.33 = bf16[2,16,32,2048]{3,1,0,2:T(8,128)(2,1)S(1)} all-to-all(bf16[2,16,32,2048]{3,1,0,2:T(8,128)(2,1)S(1)} %copy.20), channel_id=1, replica_groups=mesh['stn'=32,'tm'=8] {'stn'}, dimensions={2} | all-to-all | bytes 8388608 | tf_op jit(solution)/shard_map/all_to_all | solution.py:53
  111.6 0.0 copy-start.2
  111.6 0.6 copy.21
  112.2 0.0 copy-start.1
  112.2 2.0 copy-done.1
  114.2 1.1 slice.156
  115.3 2.5 copy.22
  117.8 2.6 collective-permute-start
  120.4 0.0 copy-done.2
  120.4 6.2 %copy.23 = bf16[2,512,1,2048]{1,3,2,0:T(8,128)(2,1)} copy(bf16[2,512,1,2048]{3,1,0,2:T(8,128)(2,1)} %bitcast.98) | data formatting | bytes 8388608 | tf_op jit(solution)/shard_map/all_to_all | solution.py:53
  126.6 0.0 collective-permute-done
  126.6 3.2 %pad_maximum_fusion = bf16[2,512,1,3008]{1,3,2,0:T(8,128)(2,1)S(1)} fusion(bf16[2,512,1,2048]{1,3,2,0:T(8,128)(2,1)} %copy.23, bf16[2,512,1,960]{1,3,2,0:T(8,128)(2,1)} %collective-permute-done), kind=kLoop, calls=%fused_computation.37 | loop fusion | flops 12320768 | bytes 12320768 | tf_op jit(solution)/shard_map/concatenate | solution.py:55
  129.9 1.8 convert.12
  131.7 18.7 %fusion.3 = f32[2,512,1,32,64]{1,4,3,2,0:T(8,128)} fusion(f32[2,512,1,47,64]{1,4,3,2,0:T(8,128)S(1)} %convert.12, f32[64]{0:T(128)S(1)} %get-tuple-element.21, f32[64]{0:T(128)S(1)} %get-tuple-element.22, f32[64]{0:T(128)S(1)} %get-tuple-element.8, f32[64]{0:T(128)S(1)} %get-tuple-element.9, f32[64]{0:T(128)S(1)} %get-tuple-element.10, ...), kind=kLoop, calls=%fused_computation.7 | loop fusion | flops 65011712 | bytes 142610432 | tf_op jit(solution)/shard_map/add | solution.py:30
  150.4 0.0 copy-start
  150.4 6.1 %fusion.18 = f32[512,32,64]{0,2,1:T(8,128)S(1)} fusion(f32[2,512,1,32,64]{1,4,3,2,0:T(8,128)} %fusion.3), kind=kOutput, calls=%fused_computation.44 | convolution fusion | flops 805363712 | bytes 8388608 | tf_op jit(solution)/shard_map/...b,bk->...k/dot_general | solution.py:42
  156.5 0.0 copy-done
  156.5 4.6 %fusion.21 = f32[512,32,64]{0,2,1:T(8,128)S(1)} fusion(f32[2,512,1,32,64]{1,4,3,2,0:T(8,128)S(1)} %copy-done), kind=kOutput, calls=%fused_computation.47 | convolution fusion | flops 805363712 | bytes 8388608 | tf_op jit(solution)/shard_map/...b,bk->...k/dot_general | solution.py:38
  161.1 4.9 %fusion.23 = bf16[1,512,1,32,64]{1,4,3,2,0:T(8,128)(2,1)S(1)} fusion(f32[512,32,64]{0,2,1:T(8,128)S(1)} %fusion.18, f32[2,512,1,32,64]{1,4,3,2,0:T(8,128)S(1)} %copy-done), kind=kOutput, calls=%fused_computation.49 | convolution fusion | flops 808509440 | bytes 10485760 | tf_op jit(solution)/shard_map/...b,bk->...k/dot_general | solution.py:41
  166.0 4.7 %fusion.22 = bf16[1,512,1,32,64]{1,4,3,2,0:T(8,128)(2,1)S(1)} fusion(f32[512,32,64]{0,2,1:T(8,128)S(1)} %fusion.21, f32[2,512,1,32,64]{1,4,3,2,0:T(8,128)S(1)} %copy-done), kind=kOutput, calls=%fused_computation.48 | convolution fusion | flops 808509440 | bytes 10485760 | tf_op jit(solution)/shard_map/...b,bk->...k/dot_general | solution.py:37
  170.8 0.4 maximum_bitcast_fusion
  171.2 2.4 copy.40
  173.6 71.9 %all_to_all.34 = bf16[64,32,2,1,512]{4,1,3,2,0:T(8,128)(2,1)S(1)} all-to-all(bf16[64,32,2,1,512]{4,1,3,2,0:T(8,128)(2,1)S(1)} %copy.40), channel_id=1, replica_groups=mesh['stn'=32,'tm'=8] {'tm'}, dimensions={0} | all-to-all | bytes 8388608 | tf_op jit(solution)/shard_map/all_to_all | solution.py:57
  245.4 6.4 %copy.46 = bf16[8,8,32,2,1,512]{5,3,2,0,1,4:T(2,128)(2,1)} copy(bf16[8,8,32,2,1,512]{5,2,3,1,0,4:T(8,128)(2,1)S(1)} %bitcast.100) | data formatting | bytes 8388608 | tf_op jit(solution)/shard_map/all_to_all | solution.py:57
  251.8 7.7 %reshape.126 = bf16[8,256,1024]{2,1,0:T(8,128)(2,1)} reshape(bf16[8,8,32,2,1,512]{5,3,2,1,0,4:T(2,128)(2,1)} %bitcast.101) | data formatting | bytes 8388608 | tf_op jit(solution)/shard_map/reshape | solution.py:59
  259.5 19.1 %fusion.56 = f32[8,1024,1024]{2,1,0:T(8,128)} fusion(bf16[8,256,1024]{2,1,0:T(8,128)(2,1)} %reshape.126), kind=kOutput, calls=%fused_computation.97 | convolution fusion | flops 4294967296 | bytes 37748736 | tf_op jit(solution)/shard_map/dot_general | solution.py:60
  278.6 19.1 %fusion.2 = (f32[1,8,1,512,512]{4,3,1,2,0:T(8,128)}, f32[1,8,1,512,512]{4,3,1,2,0:T(8,128)}) fusion(f32[8,1024,1024]{2,1,0:T(8,128)} %fusion.56), kind=kLoop, calls=%fused_computation.5 | loop fusion | flops 4194304 | bytes 50331648 | tf_op jit(solution)/shard_map/stack | solution.py:65
  297.7 9.7 %fusion = bf16[1,8,2,512,512]{4,3,1,2,0:T(8,128)(2,1)} fusion(f32[1,8,1,512,512]{4,3,1,2,0:T(8,128)} %get-tuple-element.6, f32[1,8,1,512,512]{4,3,1,2,0:T(8,128)} %get-tuple-element.5), kind=kLoop, calls=%fused_computation.1 | loop fusion | flops 12582912 | bytes 25165824 | tf_op jit(solution)/shard_map/convert_element_type | solution.py:66
  307.5 7.5 %copy.43 = bf16[1,8,2,512,512]{4,3,2,1,0:T(8,128)(2,1)} copy(bf16[1,8,2,512,512]{4,3,1,2,0:T(8,128)(2,1)} %fusion) | data formatting | bytes 16777216 | tf_op jit(solution)/shard_map/convert_element_type | solution.py:66
  (1 shorter events, 0.0 us)
Async XLA Ops:
  111.6 8.8 %copy-start.2 = (f32[16,64]{1,0:T(8,128)S(1)}, f32[16,64]{1,0:T(8,128)}, u32[]{:S(2)}) copy-start(f32[16,64]{1,0:T(8,128)} %param.3) | copy-start | bytes 12292
  112.2 2.0 copy-start.1
  117.8 8.8 %collective-permute-start = (bf16[2,512,1,960]{1,3,2,0:T(8,128)(2,1)}, bf16[2,512,1,960]{1,3,2,0:T(8,128)(2,1)}, u32[]{:S(2)}, u32[]{:S(2)}) collective-permute-start(bf16[2,512,1,960]{1,3,2,0:T(8,128)(2,1)} %copy.22), channel_id=1, source_target_pairs={{0,1},{1,2},{2,3},{3,4},{4,5},{5,6},{6,7},{8,9},{9,10},{10,11},{11... | collective-permute-start | bytes 5898248 | tf_op jit(solution)/shard_map/ppermute | solution.py:12
  150.4 6.1 %copy-start = (f32[2,512,1,32,64]{1,4,3,2,0:T(8,128)S(1)}, f32[2,512,1,32,64]{1,4,3,2,0:T(8,128)}, u32[]{:S(2)}) copy-start(f32[2,512,1,32,64]{1,4,3,2,0:T(8,128)} %fusion.3) | copy-start | bytes 25165828
where the time goes:
time: 316 us; the launch traced here: 315 us
  blocking collectives  179 us (57%)
  other arithmetic  53 us (17%)
  local copies, waits for them, and re-layouts  41 us (13%)
  matrix products  39.4 us (12%)
    all_to_all x1, blocking collectives, body(): lax.all_to_all(voltages, 'stn', split_axis=2, concat_axis=1, tiled=True)  107 us
    all_to_all x1, blocking collectives, body(): lax.all_to_all(local_spectra, 'tm', split_axis=0, concat_axis=1, tiled=True)  71.9 us
    another operation x1, other arithmetic, body(): result = jnp.stack([vis_real, vis_imag], 1) * (1.0 / total_spec)  19.1 us
    dot_general x1, matrix products, body(): lax.dot_general(matrix, matrix, (((1,), (1,)), ((0,), (0,))), preferred_e...  19.1 us
    add x1, other arithmetic, make_spectra(): filtered + fir_taps[tap_index] * frames[..., begin:begin + spec_count, :]  18.7 us
    convert_element_type x1, other arithmetic, body(): return result[None].astype(jnp.bfloat16)  9.73 us
    reshape x1, local copies, waits for them, and re-layouts, body(): matrix = gathered.reshape(channels, total_spec, 2 * inputs)  7.72 us
    convert_element_type x1, local copies, waits for them, and re-layouts, body(): return result[None].astype(jnp.bfloat16)  7.52 us
  transfers between devices with their start and end apart: 1, of which 0 were waited for; matrix products, arithmetic and copies ran while one was open for 2% of the time, Pallas kernels for 0%

commit v1 on v0

v1 whole, which is shorter than its diff:
```python
import functools
import math

import jax
import jax.numpy as jnp
import numpy as np
from jax import lax
from jax.experimental import pallas as pl
from jax.experimental.pallas import tpu as pltpu
from jax.sharding import PartitionSpec as P

MESH = pl.DeviceIdType.MESH
F32 = jnp.float32
BF16 = jnp.bfloat16

NY, NZ, NT = 4, 8, 8
STEPS = 8
ROWS = 16
LANES = NZ * ROWS
N = 2048
HIST = 1024
WIN = 1536
CH = 64
COS_ROWS = 34 * 8
SIN_ROWS = 32 * 8
AHEAD = 2
RELAY_1 = 6
NT_DIMS = (((1,), (1,)), ((), ()))


def trig_rows():
    b = np.arange(128) % CH
    rows = []
    for k in range(34):
        rows.append(np.cos(2 * np.pi * ((k * b) % CH) / CH))
    for k in range(32):
        rows.append(np.sin(2 * np.pi * ((k * b) % CH) / CH))
    table = np.stack(rows) / math.sqrt(CH)
    return np.repeat(table, 8, axis=0).astype(np.float32)


def comm_kernel(
    v_ref, taps_ref, trig_ref, out_ref,
    vbuf, sb, recv, jx, spec, w_hi, w_lo, ppad, t16, rc, rs, relay,
    v_sem, zs, zr, fr, rr, hs, hr, xs, xr, xl,
):
    stn = lax.axis_index("stn")
    tm = lax.axis_index("tm")
    y = lax.div(stn, NZ)
    z = lax.rem(stn, NZ)

    barrier = pltpu.get_barrier_semaphore()

    def greet_stn(i, _):
        pl.semaphore_signal(
            barrier, inc=1, device_id=(lax.rem(stn + i, NY * NZ), tm), device_id_type=MESH
        )
        return 0

    def greet_tm(i, _):
        pl.semaphore_signal(
            barrier, inc=1, device_id=(stn, lax.rem(tm + i, NT)), device_id_type=MESH
        )
        return 0

    def v_copy(i):
        qt, h = i // 2, i % 2
        return pltpu.make_async_copy(
            v_ref.at[:, pl.ds(h * 8, 8), pl.ds(qt * 16, 16), :], vbuf.at[i], v_sem.at[i]
        )

    for i in range(4):
        v_copy(i).start()
    lax.fori_loop(1, NY * NZ, greet_stn, 0)
    lax.fori_loop(1, NT, greet_tm, 0)

    def relayout(j):
        d, h = lax.div(j, 2), lax.rem(j, 2)
        yt = lax.rem(y + d, NY)
        at = lax.div(yt, 2) * 2 + h
        odd = lax.rem(yt, 2)
        o = lax.broadcasted_iota(jnp.int32, (LANES, 256), 0)
        c = lax.broadcasted_iota(jnp.int32, (LANES, 256), 1)
        want = ((o >> 3) & 1) * 128 + (o & 7) * 16 + odd * 8 + (o >> 4)
        perm = jnp.where(c == want, 1.0, 0.0).astype(BF16)
        for lane in range(0, N, 512):
            x = vbuf[at, :, :, :, lane : lane + 512].reshape(256, 512)
            turned = jnp.dot(perm, x, preferred_element_type=F32).astype(BF16)
            sb[j, :, :, lane : lane + 512] = turned.reshape(NZ, ROWS, 512)

    def z_copy(j, dz, first=0, count=N, sems=None):
        zt = lax.rem(z + dz, NZ)
        yt = lax.rem(y + lax.div(j, 2), NY)
        return pltpu.make_async_remote_copy(
            src_ref=sb.at[j, zt, :, pl.ds(first, count)],
            dst_ref=recv.at[j, z, :, pl.ds(HIST + first, count)],
            send_sem=zs.at[j],
            recv_sem=zr.at[j],
            device_id=(yt * NZ + zt, tm),
            device_id_type=MESH,
        )

    def own_copy(j):
        return pltpu.make_async_copy(
            sb.at[j, z], recv.at[j, z, :, pl.ds(HIST, N)], zr.at[j]
        )

    def relay_copy(j):
        zt = lax.rem(z + 4, NZ)
        return pltpu.make_async_remote_copy(
            src_ref=sb.at[j, zt, :, pl.ds(1024, 1024)],
            dst_ref=relay.at[j],
            send_sem=zs.at[j],
            recv_sem=rr.at[j],
            device_id=(y * NZ + lax.rem(z + RELAY_1, NZ), tm),
            device_id_type=MESH,
        )

    def forward_copy(j):
        source = lax.rem(z + NZ - RELAY_1, NZ)
        yt = lax.rem(y + lax.div(j, 2), NY)
        return pltpu.make_async_remote_copy(
            src_ref=relay.at[j],
            dst_ref=recv.at[j, source, :, pl.ds(HIST + 1024, 1024)],
            send_sem=fr.at[j],
            recv_sem=zr.at[j],
            device_id=(yt * NZ + lax.rem(z + 12 - RELAY_1, NZ), tm),
            device_id_type=MESH,
        )

    def send_step(j):
        relayout(j)
        if RELAY_1:
            relay_copy(j).start()
            z_copy(j, 4, 0, 1024).start()
        else:
            z_copy(j, 4).start()
        for dz in (3, 5, 2, 6, 1, 7):
            z_copy(j, dz).start()

        @pl.when(j < 2)
        def _():
            own_copy(j).start()

        @pl.when(j >= 2)
        def _():
            z_copy(j, 0).start()

    def forward(j):
        if RELAY_1:
            relay_copy(j).wait_recv()
            forward_copy(j).start()

    def wait_step(j):
        whole = recv.at[j, :, :, pl.ds(HIST, N)]
        pltpu.make_async_copy(whole, whole, zr.at[j]).wait()

    def halo_copy(j):
        return pltpu.make_async_remote_copy(
            src_ref=recv.at[j, :, :, pl.ds(N, HIST)],
            dst_ref=recv.at[j, :, :, pl.ds(0, HIST)],
            send_sem=hs.at[j],
            recv_sem=hr.at[j],
            device_id=(stn, lax.rem(tm + 1, NT)),
            device_id_type=MESH,
        )

    def slot_of(j):
        return lax.rem(y + NY - lax.div(j, 2), NY) * 2 + lax.rem(j, 2)

    def x_copy(j, gp, o):
        to = lax.rem(tm + o, NT)
        return pltpu.make_async_remote_copy(
            src_ref=spec.at[j, gp, pl.ds(to * 8, 8)],
            dst_ref=out_ref.at[tm, slot_of(j), gp],
            send_sem=xs.at[j],
            recv_sem=xr.at[j],
            device_id=(stn, to),
            device_id_type=MESH,
        )

    def x_own(j, gp):
        return pltpu.make_async_copy(
            spec.at[j, gp, pl.ds(tm * 8, 8)], out_ref.at[tm, slot_of(j), gp], xl.at[j]
        )

    def turn_complex(j, lane):
        o = lax.broadcasted_iota(jnp.int32, (LANES, LANES), 0)
        c = lax.broadcasted_iota(jnp.int32, (LANES, LANES), 1)
        im = (o >> 3) & 1
        sign = (1 - 2 * im).astype(F32)
        turn = jnp.where(c == o + 8 - 16 * im, sign, 0.0).astype(BF16)
        x = recv[j, :, :, lane : lane + 512].reshape(LANES, 512)
        jx[:, lane : lane + 512] = jnp.dot(turn, x, preferred_element_type=F32).astype(BF16)

    def spectra(j, gp):
        lo0 = 1024 * gp
        lo1 = lo0 + 512

        def both(w0, w1, x):
            hi = lax.dot_general(w_hi[w0:w1, :], x, NT_DIMS, preferred_element_type=F32)
            lo = lax.dot_general(w_lo[w0:w1, :], x, NT_DIMS, preferred_element_type=F32)
            return hi + lo

        x = jnp.concatenate(
            [
                recv[j, :, :, lo0 : lo0 + WIN].reshape(LANES, WIN),
                recv[j, :, :, lo1 : lo1 + WIN].reshape(LANES, WIN),
            ],
            axis=0,
        )
        rc[...] = both(0, COS_ROWS, x)
        x = jnp.concatenate([jx[:, lo0 : lo0 + WIN], jx[:, lo1 : lo1 + WIN]], axis=0)
        rs[...] = both(COS_ROWS, COS_ROWS + SIN_ROWS, x)

        def put(k, a):
            tile = jnp.concatenate([a[:, :128], a[:, 128:]], axis=0)
            spec[j, gp, k] = tile.astype(BF16)

        put(0, rc[0:8, :])
        put(32, rc[256:264, :])
        for k in range(1, 32):
            c = rc[8 * k : 8 * k + 8, :]
            s = rs[8 * k : 8 * k + 8, :]
            put(k, c + s)
            put(64 - k, c - s)

    def send_spectra(j, gp):
        x_own(j, gp).start()

        def start(o, _):
            x_copy(j, gp, o).start()
            return 0

        lax.fori_loop(1, NT, start, 0)

    for i in range(4):
        v_copy(i).wait()
    relayout(0)
    pl.semaphore_wait(barrier, NY * NZ - 1 + NT - 1)

    def prime(j, _):
        send_step(j)
        return 0

    lax.fori_loop(0, AHEAD, prime, 0)

    half = lax.broadcasted_iota(jnp.int32, (16, 128), 1) < CH
    taps = jnp.concatenate([taps_ref[...], taps_ref[...]], axis=1)
    ppad[...] = jnp.zeros_like(ppad)
    ppad[8:24, :] = jnp.where(half, taps, 0.0)
    ppad[9:25, :] = ppad[9:25, :] + jnp.where(half, 0.0, taps)
    for i in range(WIN // 128):
        tile = ppad[24 - 2 * i : 32 - 2 * i, :]
        t16[:, 128 * i : 128 * i + 128] = jnp.concatenate([tile, tile], axis=0)

    def weights(i, _):
        rows = pl.ds(pl.multiple_of(i * 16, 16), 16)
        trig = trig_ref[rows, :]
        for t in range(WIN // 128):
            lanes = slice(128 * t, 128 * t + 128)
            w = t16[:, lanes] * trig
            hi = w.astype(BF16)
            w_hi[rows, lanes] = hi
            w_lo[rows, lanes] = (w - hi.astype(F32)).astype(BF16)
        return 0

    lax.fori_loop(0, (COS_ROWS + SIN_ROWS) // 16, weights, 0)

    forward(0)

    def step(j, _):
        @pl.when(j + AHEAD < STEPS)
        def _():
            send_step(j + AHEAD)

        wait_step(j)

        @pl.when(tm < NT - 1)
        def _():
            halo_copy(j).start()

        for lane in range(HIST, HIST + N, 512):
            turn_complex(j, lane)
        spectra(j, 1)
        send_spectra(j, 1)

        @pl.when(j + 1 < STEPS)
        def _():
            forward(j + 1)

        @pl.when(tm > 0)
        def _():
            halo_copy(j).wait_recv()

        @pl.when(tm == 0)
        def _():
            recv[j, :, :, 0:HIST] = jnp.zeros((NZ, ROWS, HIST), BF16)

        for lane in range(0, HIST, 512):
            turn_complex(j, lane)
        spectra(j, 0)
        send_spectra(j, 0)
        return 0

    lax.fori_loop(0, STEPS, step, 0)

    def finish(j, _):
        @pl.when(j < 2)
        def _():
            part = sb.at[j, pl.ds(0, NZ - 1)]
            pltpu.make_async_copy(part, part, zs.at[j]).wait()

        @pl.when(j >= 2)
        def _():
            part = sb.at[j]
            pltpu.make_async_copy(part, part, zs.at[j]).wait()

        if RELAY_1:
            forward_copy(j).wait_send()

        @pl.when(tm < NT - 1)
        def _():
            halo_copy(j).wait_send()

        mine = spec.at[j, :, pl.ds(0, 8)]
        pltpu.make_async_copy(mine, mine, xl.at[j]).wait()
        others = spec.at[j, :, pl.ds(0, 56)]
        pltpu.make_async_copy(others, others, xs.at[j]).wait()
        pltpu.make_async_copy(others, others, xr.at[j]).wait()
        return 0

    lax.fori_loop(0, STEPS, finish, 0)


def gram_kernel(x_ref, order_ref, out_ref):
    def inputs(yy):
        a = jnp.concatenate(
            [
                x_ref[:, 2 * yy, :, 0].reshape(256, 128),
                x_ref[:, 2 * yy + 1, :, 0].reshape(256, 128),
            ],
            axis=1,
        )
        return lax.dot_general(
            order_ref[...], a, NT_DIMS, preferred_element_type=F32
        ).astype(BF16)

    parts = [inputs(yy) for yy in range(NY)]
    re = jnp.concatenate([t[:128] for t in parts], axis=0)
    im = jnp.concatenate([t[128:] for t in parts], axis=0)
    u = jnp.concatenate([re, im], axis=1)
    w = jnp.concatenate([im, -re], axis=1)
    scale = 1.0 / 256
    real = lax.dot_general(u, u, NT_DIMS, preferred_element_type=F32)
    out_ref[0, 0, 0] = (real * scale).astype(BF16)
    imag = lax.dot_general(w, u, NT_DIMS, preferred_element_type=F32)
    out_ref[0, 0, 1] = (imag * scale).astype(BF16)


def input_order():
    m = np.zeros((256, 256), np.float32)
    for ri in range(2):
        for zz in range(8):
            for h in range(2):
                for r in range(8):
                    m[ri * 128 + zz * 16 + h * 8 + r, h * 128 + zz * 16 + ri * 8 + r] = 1.0
    return m


def body(voltages, fir_taps):
    dma = pltpu.SemaphoreType.DMA
    any_space = pl.BlockSpec(memory_space=pl.ANY)
    in_vmem = pl.BlockSpec(memory_space=pltpu.VMEM)
    gathered = pl.pallas_call(
        comm_kernel,
        out_shape=jax.ShapeDtypeStruct((NT, STEPS, 2, 8, 16, 128), BF16),
        in_specs=[any_space, in_vmem, in_vmem],
        out_specs=any_space,
        scratch_shapes=[
            pltpu.VMEM((4, 2, 8, 16, N), BF16),
            pltpu.VMEM((STEPS, NZ, ROWS, N), BF16),
            pltpu.VMEM((STEPS, NZ, ROWS, HIST + N), BF16),
            pltpu.VMEM((LANES, HIST + N), BF16),
            pltpu.VMEM((STEPS, 2, CH, 16, 128), BF16),
            pltpu.VMEM((COS_ROWS + SIN_ROWS, WIN), BF16),
            pltpu.VMEM((COS_ROWS + SIN_ROWS, WIN), BF16),
            pltpu.VMEM((32, 128), F32),
            pltpu.VMEM((16, WIN), F32),
            pltpu.VMEM((COS_ROWS, 256), F32),
            pltpu.VMEM((SIN_ROWS, 256), F32),
            pltpu.VMEM((STEPS, ROWS, 1024), BF16),
            dma((4,)),
        ]
        + [dma((STEPS,))] * 9,
        compiler_params=pltpu.CompilerParams(
            collective_id=0, has_side_effects=True, vmem_limit_bytes=48 * 2**20
        ),
        name="exchange",
    )(voltages, fir_taps, jnp.asarray(trig_rows()))
    return pl.pallas_call(
        gram_kernel,
        grid=(8,),
        out_shape=jax.ShapeDtypeStruct((1, 8, 2, 512, 512), BF16),
        in_specs=[
            pl.BlockSpec((NT, STEPS, 2, 1, 16, 128), lambda k: (0, 0, 0, k, 0, 0)),
            pl.BlockSpec((256, 256), lambda k: (0, 0)),
        ],
        out_specs=pl.BlockSpec((1, 1, 2, 512, 512), lambda k: (0, k, 0, 0, 0)),
        compiler_params=pltpu.CompilerParams(vmem_limit_bytes=32 * 2**20),
        name="gram",
    )(gathered, jnp.asarray(input_order(), BF16))


def solution(mesh):
    return jax.shard_map(
        body,
        mesh=mesh,
        in_specs=(P(None, "stn", None, "tm"), P()),
        out_specs=P("stn", "tm", None, None, None),
        check_vma=False,
    )
```

time: 316 us -> 145 us (0.46)
  blocking collectives: 179 us -> 0 us
  Pallas kernels: 0 us -> 141 us
  other arithmetic: 53 us -> 0 us
  matrix products: 39.4 us -> 0 us
  local copies, waits for them, and re-layouts: 41 us -> 1.65 us
    all_to_all x2 -> x0, blocking collectives: 179 us -> none  [the longest x1 107 us: body(): lax.all_to_all(voltages, 'stn', split_axis=2, concat_axis=1, tiled=True)]
    pallas_call x0 -> x2, Pallas kernels: none -> 141 us  [the longest x1 131 us: body(): pl.pallas_call(comm_kernel, out_shape=jax.ShapeDtypeStruct((NT, STEPS, 2,...]
    dot_general x5 -> x0, matrix products: 39.4 us -> none  [the longest x1 19.1 us: body(): lax.dot_general(matrix, matrix, (((1,), (1,)), ((0,), (0,))), preferred_e...]
    another operation x1 -> x0, other arithmetic: 19.1 us -> none  [body(): result = jnp.stack([vis_real, vis_imag], 1) * (1.0 / total_spec)]
    add x1 -> x0, other arithmetic: 18.7 us -> none  [make_spectra(): filtered + fir_taps[tap_index] * frames[..., begin:begin + spec_count, :]]
    all_to_all x3 -> x0, local copies, waits for them, and re-layouts: 13.2 us -> none  [the longest x2 6.81 us: body(): lax.all_to_all(voltages, 'stn', split_axis=2, concat_axis=1, tiled=True)]
    convert_element_type x3 -> x0, other arithmetic: 11.9 us -> none  [the longest x1 9.73 us: body(): return result[None].astype(jnp.bfloat16)]
    convert_element_type x2 -> x0, local copies, waits for them, and re-layouts: 9.91 us -> none  [the longest x1 7.52 us: body(): return result[None].astype(jnp.bfloat16)]
  transfers between devices with their start and end apart: 1 -> 0, of which waited for: 0 -> 0; matrix products, arithmetic and copies ran while one was open for 2% -> 0% of each run, Pallas kernels for 0% -> 0%
where the time goes in v1:
time: 145 us; the launch traced here: 143 us
  Pallas kernels  141 us (97%)
  local copies, waits for them, and re-layouts  1.65 us (1%)
    pallas_call x1, Pallas kernels, body(): pl.pallas_call(comm_kernel, out_shape=jax.ShapeDtypeStruct((NT, STEPS, 2,...  131 us
    pallas_call x1, Pallas kernels, body(): pl.pallas_call(gram_kernel, grid=(8,), out_shape=jax.ShapeDtypeStruct((1,...  9.67 us

profile of v1, /device:TPU:32, one launch (start us, length us, event | category | flops | bytes accessed | tf_op | source)
XLA Modules:
  0.0 142.8 jit_solution(16494784753668856771)
XLA Ops:
  0.0 0.0 copy-start
  0.0 1.0 copy-done
  1.0 0.0 copy-start.2
  1.0 0.7 copy-done.2
  1.7 0.0 copy-start.1
  1.7 131.5 %exchange.1.x_ref = bf16[8,8,2,8,16,128]{5,4,3,2,1,0:T(8,128)(2,1)S(1)} custom-call(bf16[2,16,32,2048]{3,2,1,0:T(8,128)(2,1)} %v_ref.1, f32[16,64]{1,0:T(8,128)S(1)} %copy-done.2, f32[528,128]{1,0:T(8,128)S(1)} %copy-done), custom_call_target="tpu_custom_call" | custom-call | tf_op jit(solution)/shard_map/exchange/pallas_call | solution.py:375
  133.2 0.0 copy-done.1
  133.2 9.7 %gram.1 = bf16[1,8,2,512,512]{4,3,2,1,0:T(8,128)(2,1)} custom-call(bf16[8,8,2,8,16,128]{5,4,3,2,1,0:T(8,128)(2,1)S(1)} %exchange.1.x_ref, bf16[256,256]{1,0:T(8,128)(2,1)S(1)} %copy-done.1), custom_call_target="tpu_custom_call" | custom-call | tf_op jit(solution)/shard_map/gram/pallas_call | solution.py:401
Async XLA Ops:
  0.0 1.0 copy-start
  1.0 0.7 copy-start.2
  1.7 131.5 %copy-start.1 = (bf16[256,256]{1,0:T(8,128)(2,1)S(1)}, bf16[256,256]{1,0:T(8,128)(2,1)}, u32[]{:S(2)}) copy-start(bf16[256,256]{1,0:T(8,128)(2,1)} %constant.5.clone.order_ref) | copy-start | bytes 393220

commit v2 on v1

v2 whole, which is shorter than its diff:
```python
import functools
import math

import jax
import jax.numpy as jnp
import numpy as np
from jax import lax
from jax.experimental import pallas as pl
from jax.experimental.pallas import tpu as pltpu
from jax.sharding import PartitionSpec as P

MESH = pl.DeviceIdType.MESH
F32 = jnp.float32
BF16 = jnp.bfloat16

NY, NZ, NT = 4, 8, 8
STEPS = 8
ROWS = 16
LANES = NZ * ROWS
N = 2048
HIST = 1024
WIN = 1536
CH = 64
COS_ROWS = 34 * 8
SIN_ROWS = 32 * 8
AHEAD = 2
FIRST = 6
ORDER = (1, 7, 2, 6, 3, 5, 4, 0)
NT_DIMS = (((1,), (1,)), ((), ()))


def trig_rows():
    b = np.arange(128) % CH
    rows = []
    for k in range(34):
        rows.append(np.cos(2 * np.pi * ((k * b) % CH) / CH))
    for k in range(32):
        rows.append(np.sin(2 * np.pi * ((k * b) % CH) / CH))
    table = np.stack(rows) / math.sqrt(CH)
    return np.repeat(table, 8, axis=0).astype(np.float32)


def comm_kernel(
    v_ref, taps_hbm, trig_hbm, u_ref,
    vbuf, taps_ref, trig_ref, sb, recv, jx, spec, xg, ub, zbuf,
    w_hi, w_lo, ppad, t16, rc, rs,
    v_sem, c_sem, zs, zr, hs, hr, xs, xr, us,
):
    stn = lax.axis_index("stn")
    tm = lax.axis_index("tm")
    y = lax.div(stn, NZ)
    z = lax.rem(stn, NZ)

    barrier = pltpu.get_barrier_semaphore()

    def greet_stn(i, _):
        pl.semaphore_signal(
            barrier, inc=1, device_id=(lax.rem(stn + i, NY * NZ), tm), device_id_type=MESH
        )
        return 0

    def greet_tm(i, _):
        pl.semaphore_signal(
            barrier, inc=1, device_id=(stn, lax.rem(tm + i, NT)), device_id_type=MESH
        )
        return 0

    def v_copy(i):
        qt, h = i // 2, i % 2
        return pltpu.make_async_copy(
            v_ref.at[:, pl.ds(h * 8, 8), pl.ds(qt * 16, 16), :], vbuf.at[i], v_sem.at[i]
        )

    taps_copy = pltpu.make_async_copy(taps_hbm, taps_ref, c_sem.at[0])
    trig_copy = pltpu.make_async_copy(trig_hbm, trig_ref, c_sem.at[1])
    for i in range(4):
        v_copy(i).start()
    taps_copy.start()
    trig_copy.start()
    lax.fori_loop(1, NY * NZ, greet_stn, 0)
    lax.fori_loop(1, NT, greet_tm, 0)

    def relayout(j, put):
        d, h = lax.div(j, 2), lax.rem(j, 2)
        yt = lax.rem(y + d, NY)
        at = lax.div(yt, 2) * 2 + h
        odd = lax.rem(yt, 2)
        o = lax.broadcasted_iota(jnp.int32, (LANES, 256), 0)
        c = lax.broadcasted_iota(jnp.int32, (LANES, 256), 1)
        want = ((o >> 3) & 1) * 128 + (o & 7) * 16 + odd * 8 + (o >> 4)
        perm = jnp.where(c == want, 1.0, 0.0).astype(BF16)
        for lane in range(0, N, 512):
            x = vbuf[at, :, :, :, lane : lane + 512].reshape(256, 512)
            turned = jnp.dot(perm, x, preferred_element_type=F32).astype(BF16)
            put(lane, turned.reshape(NZ, ROWS, 512))

    def z_target(j, dz):
        zt = lax.rem(z + dz, NZ)
        yt = lax.rem(y + lax.div(j, 2), NY)
        return zt, (yt * NZ + zt, tm)

    def z_copy(j, dz):
        zt, to = z_target(j, dz)
        return pltpu.make_async_remote_copy(
            src_ref=sb.at[j, zt],
            dst_ref=recv.at[j, z, :, pl.ds(HIST, N)],
            send_sem=zs.at[j],
            recv_sem=zr.at[j],
            device_id=to,
            device_id_type=MESH,
        )

    def own_copy(j):
        return pltpu.make_async_copy(
            sb.at[j, z], recv.at[j, z, :, pl.ds(HIST, N)], zr.at[j]
        )

    def late_copy(j, dz):
        zt, to = z_target(j, dz)
        ri = lax.rem(j, 2)
        at = pl.multiple_of(y * 128 + z * 16, 16)
        return pltpu.make_async_remote_copy(
            src_ref=zbuf.at[zt, ri],
            dst_ref=u_ref.at[ri, pl.ds(at, 16), :],
            send_sem=zs.at[j],
            recv_sem=zr.at[j],
            device_id=to,
            device_id_type=MESH,
        )

    def send_step(j):
        def put(lane, tile):
            sb[j, :, :, lane : lane + 512] = tile

        relayout(j, put)
        for dz in ORDER[:-1]:
            z_copy(j, dz).start()

        @pl.when(j < 2)
        def _():
            own_copy(j).start()

        @pl.when(j >= 2)
        def _():
            z_copy(j, 0).start()

    def send_late(j):
        for dz in ORDER:
            late_copy(j, dz).start()

    def wait_step(j):
        whole = recv.at[j, :, :, pl.ds(HIST, N)]
        pltpu.make_async_copy(whole, whole, zr.at[j]).wait()

    def halo_copy(j):
        return pltpu.make_async_remote_copy(
            src_ref=recv.at[j, :, :, pl.ds(N, HIST)],
            dst_ref=recv.at[j, :, :, pl.ds(0, HIST)],
            send_sem=hs.at[j],
            recv_sem=hr.at[j],
            device_id=(stn, lax.rem(tm + 1, NT)),
            device_id_type=MESH,
        )

    def send_halo(j):
        @pl.when(tm < NT - 1)
        def _():
            halo_copy(j).start()

    def wait_halo(j):
        @pl.when(tm > 0)
        def _():
            halo_copy(j).wait_recv()

        @pl.when(tm == 0)
        def _():
            recv[j, :, :, 0:HIST] = jnp.zeros((NZ, ROWS, HIST), BF16)

    def x_copy(j, gp, o):
        to = lax.rem(tm + o, NT)
        return pltpu.make_async_remote_copy(
            src_ref=spec.at[j, gp, pl.ds(to * 8, 8)],
            dst_ref=xg.at[j, tm, gp],
            send_sem=xs.at[j],
            recv_sem=xr.at[j],
            device_id=(stn, to),
            device_id_type=MESH,
        )

    def x_own(j, gp):
        return pltpu.make_async_copy(
            spec.at[j, gp, pl.ds(tm * 8, 8)], xg.at[j, tm, gp], xr.at[j]
        )

    def turn_complex(j, lane):
        o = lax.broadcasted_iota(jnp.int32, (LANES, LANES), 0)
        c = lax.broadcasted_iota(jnp.int32, (LANES, LANES), 1)
        im = (o >> 3) & 1
        sign = (1 - 2 * im).astype(F32)
        turn = jnp.where(c == o + 8 - 16 * im, sign, 0.0).astype(BF16)
        x = recv[j, :, :, lane : lane + 512].reshape(LANES, 512)
        jx[:, lane : lane + 512] = jnp.dot(turn, x, preferred_element_type=F32).astype(BF16)

    def spectra(j, gp):
        lo0 = 1024 * gp
        lo1 = lo0 + 512

        def both(w0, w1, x):
            hi = lax.dot_general(w_hi[w0:w1, :], x, NT_DIMS, preferred_element_type=F32)
            lo = lax.dot_general(w_lo[w0:w1, :], x, NT_DIMS, preferred_element_type=F32)
            return hi + lo

        x = jnp.concatenate(
            [
                recv[j, :, :, lo0 : lo0 + WIN].reshape(LANES, WIN),
                recv[j, :, :, lo1 : lo1 + WIN].reshape(LANES, WIN),
            ],
            axis=0,
        )
        rc[...] = both(0, COS_ROWS, x)
        x = jnp.concatenate([jx[:, lo0 : lo0 + WIN], jx[:, lo1 : lo1 + WIN]], axis=0)
        rs[...] = both(COS_ROWS, COS_ROWS + SIN_ROWS, x)

        def put(k, a):
            tile = jnp.concatenate([a[:, :128], a[:, 128:]], axis=0)
            spec[j, gp, k] = tile.astype(BF16)

        put(0, rc[0:8, :])
        put(32, rc[256:264, :])
        for k in range(1, 32):
            c = rc[8 * k : 8 * k + 8, :]
            s = rs[8 * k : 8 * k + 8, :]
            put(k, c + s)
            put(64 - k, c - s)

    def send_spectra(j, gp):
        def start(o, _):
            x_copy(j, gp, o).start()
            return 0

        lax.fori_loop(1, NT, start, 0)
        x_own(j, gp).start()

    def filterbank(j):
        for lane in range(HIST, HIST + N, 512):
            turn_complex(j, lane)
        spectra(j, 1)
        send_spectra(j, 1)
        wait_halo(j)
        for lane in range(0, HIST, 512):
            turn_complex(j, lane)
        spectra(j, 0)
        send_spectra(j, 0)

    def wait_spectra(j):
        pltpu.make_async_copy(spec.at[j], spec.at[j], xr.at[j]).wait()

    def turn_pair(d, want, put):
        wait_spectra(2 * d)
        wait_spectra(2 * d + 1)
        c = lax.broadcasted_iota(jnp.int32, (256, 256), 1)
        perm = jnp.where(c == want, 1.0, 0.0).astype(BF16)

        def channel(k, _):
            a = jnp.concatenate(
                [
                    xg[2 * d, :, :, k].reshape(256, LANES),
                    xg[2 * d + 1, :, :, k].reshape(256, LANES),
                ],
                axis=1,
            )
            t = lax.dot_general(perm, a, NT_DIMS, preferred_element_type=F32)
            put(pl.ds(pl.multiple_of(k * 256, 256), 256), t.astype(BF16))
            return 0

        lax.fori_loop(0, 8, channel, 0)

    def u_copy(d):
        at = pl.multiple_of(lax.rem(y + NY - d, NY) * 128, 128)
        return pltpu.make_async_copy(ub.at[d], u_ref.at[:, pl.ds(at, 128), :], us.at[d])

    def turn_early(d):
        o = lax.broadcasted_iota(jnp.int32, (256, 256), 0)
        want = ((o >> 3) & 1) * 128 + ((o >> 4) & 7) * 16 + (o >> 7) * 8 + (o & 7)

        def put(lanes, t):
            ub[d, :, :, lanes] = t.reshape(2, 128, 256)

        turn_pair(d, want, put)
        u_copy(d).start()

    def turn_late():
        o = lax.broadcasted_iota(jnp.int32, (256, 256), 0)
        want = ((o >> 3) & 1) * 128 + (o >> 5) * 16 + ((o >> 4) & 1) * 8 + (o & 7)

        def put(lanes, t):
            zbuf[:, :, :, lanes] = t.reshape(NZ, 2, 16, 256)

        turn_pair(3, want, put)

    for i in range(4):
        v_copy(i).wait()
    pl.semaphore_wait(barrier, NY * NZ - 1 + NT - 1)

    def prime(j, _):
        send_step(j)
        return 0

    lax.fori_loop(0, AHEAD, prime, 0)

    def prime_late(j, _):
        def put(lane, tile):
            recv[j, :, :, HIST + lane : HIST + lane + 512] = tile

        relayout(j, put)
        send_halo(j)
        return 0

    lax.fori_loop(FIRST, STEPS, prime_late, 0)

    taps_copy.wait()
    trig_copy.wait()
    half = lax.broadcasted_iota(jnp.int32, (16, 128), 1) < CH
    taps = jnp.concatenate([taps_ref[...], taps_ref[...]], axis=1)
    ppad[...] = jnp.zeros_like(ppad)
    ppad[8:24, :] = jnp.where(half, taps, 0.0)
    ppad[9:25, :] = ppad[9:25, :] + jnp.where(half, 0.0, taps)
    for i in range(WIN // 128):
        tile = ppad[24 - 2 * i : 32 - 2 * i, :]
        t16[:, 128 * i : 128 * i + 128] = jnp.concatenate([tile, tile], axis=0)

    def weights(i, _):
        rows = pl.ds(pl.multiple_of(i * 16, 16), 16)
        trig = trig_ref[rows, :]
        for t in range(WIN // 128):
            lanes = slice(128 * t, 128 * t + 128)
            w = t16[:, lanes] * trig
            hi = w.astype(BF16)
            w_hi[rows, lanes] = hi
            w_lo[rows, lanes] = (w - hi.astype(F32)).astype(BF16)
        return 0

    lax.fori_loop(0, (COS_ROWS + SIN_ROWS) // 16, weights, 0)

    def step(i, _):
        j = jnp.where(i < 2, FIRST + i, i - 2)

        @pl.when(i >= 2)
        def _():
            @pl.when(j + AHEAD < FIRST)
            def _():
                send_step(j + AHEAD)

            @pl.when(j + AHEAD >= FIRST)
            def _():
                send_late(j + AHEAD)

            wait_step(j)
            send_halo(j)

        filterbank(j)

        @pl.when(j == LATE_AT)
        def _():
            turn_late()

        @pl.when((j == 3) | (j == 5))
        def _():
            turn_early(lax.div(j - 3, 2))

        return 0

    lax.fori_loop(0, STEPS, step, 0)
    turn_early(2)

    def finish(j, _):
        @pl.when(j < 2)
        def _():
            part = sb.at[j, pl.ds(0, NZ - 1)]
            pltpu.make_async_copy(part, part, zs.at[j]).wait()

        @pl.when(j >= 2)
        def _():
            part = sb.at[0]
            pltpu.make_async_copy(part, part, zs.at[j]).wait()

        @pl.when(j >= FIRST)
        def _():
            wait_step(j)

        @pl.when(tm < NT - 1)
        def _():
            halo_copy(j).wait_send()

        others = spec.at[j, :, pl.ds(0, 56)]
        pltpu.make_async_copy(others, others, xs.at[j]).wait()
        return 0

    lax.fori_loop(0, STEPS, finish, 0)
    for d in range(3):
        u_copy(d).wait()


LATE_AT = 1


def gram_kernel(u_ref, out_ref):
    re, im = u_ref[0], u_ref[1]
    u = jnp.concatenate([re, im], axis=1)
    w = jnp.concatenate([im, -re], axis=1)
    scale = 1.0 / 256
    real = lax.dot_general(u, u, NT_DIMS, preferred_element_type=F32)
    out_ref[0, 0, 0] = (real * scale).astype(BF16)
    imag = lax.dot_general(w, u, NT_DIMS, preferred_element_type=F32)
    out_ref[0, 0, 1] = (imag * scale).astype(BF16)


def body(voltages, fir_taps):
    dma = pltpu.SemaphoreType.DMA
    any_space = pl.BlockSpec(memory_space=pl.ANY)
    gathered = pl.pallas_call(
        comm_kernel,
        out_shape=jax.ShapeDtypeStruct((2, 512, 8 * 256), BF16),
        in_specs=[pl.BlockSpec(memory_space=pltpu.HBM)] * 3,
        out_specs=any_space,
        scratch_shapes=[
            pltpu.VMEM((4, 2, 8, 16, N), BF16),
            pltpu.VMEM((16, CH), F32),
            pltpu.VMEM((COS_ROWS + SIN_ROWS, 128), F32),
            pltpu.VMEM((FIRST, NZ, ROWS, N), BF16),
            pltpu.VMEM((STEPS, NZ, ROWS, HIST + N), BF16),
            pltpu.VMEM((LANES, HIST + N), BF16),
            pltpu.VMEM((STEPS, 2, CH, 16, 128), BF16),
            pltpu.VMEM((STEPS, NT, 2, 8, 16, 128), BF16),
            pltpu.VMEM((3, 2, 128, 8 * 256), BF16),
            pltpu.VMEM((NZ, 2, 16, 8 * 256), BF16),
            pltpu.VMEM((COS_ROWS + SIN_ROWS, WIN), BF16),
            pltpu.VMEM((COS_ROWS + SIN_ROWS, WIN), BF16),
            pltpu.VMEM((32, 128), F32),
            pltpu.VMEM((16, WIN), F32),
            pltpu.VMEM((COS_ROWS, 256), F32),
            pltpu.VMEM((SIN_ROWS, 256), F32),
            dma((4,)),
            dma((2,)),
        ]
        + [dma((STEPS,))] * 6
        + [dma((3,))],
        compiler_params=pltpu.CompilerParams(
            collective_id=0, has_side_effects=True, vmem_limit_bytes=48 * 2**20
        ),
        name="exchange",
    )(voltages, fir_taps, jnp.asarray(trig_rows()))
    return pl.pallas_call(
        gram_kernel,
        grid=(8,),
        out_shape=jax.ShapeDtypeStruct((1, 8, 2, 512, 512), BF16),
        in_specs=[pl.BlockSpec((2, 512, 256), lambda k: (0, 0, k))],
        out_specs=pl.BlockSpec((1, 1, 2, 512, 512), lambda k: (0, k, 0, 0, 0)),
        compiler_params=pltpu.CompilerParams(vmem_limit_bytes=16 * 2**20),
        name="gram",
    )(gathered)


def solution(mesh):
    return jax.shard_map(
        body,
        mesh=mesh,
        in_specs=(P(None, "stn", None, "tm"), P()),
        out_specs=P("stn", "tm", None, None, None),
        check_vma=False,
    )
```

time: 145 us -> 114 us (0.79); the launches traced: 143 us -> 114 us
  Pallas kernels: 141 us -> 112 us
    pallas_call x1, Pallas kernels: 131 us -> 104 us  [body(): pl.pallas_call(comm_kernel, out_shape=jax.ShapeDtypeStruct((2, 512, 8 * 2...]
    pallas_call x1, Pallas kernels: 9.67 us -> 8.01 us  [body(): pl.pallas_call(gram_kernel, grid=(8,), out_shape=jax.ShapeDtypeStruct((1,...]
where the time goes in v2:
time: 114 us
  Pallas kernels  112 us (98%)
  local copies, waits for them, and re-layouts  1.65 us (1%)
    pallas_call x1, Pallas kernels, body(): pl.pallas_call(comm_kernel, out_shape=jax.ShapeDtypeStruct((2, 512, 8 * 2...  104 us
    pallas_call x1, Pallas kernels, body(): pl.pallas_call(gram_kernel, grid=(8,), out_shape=jax.ShapeDtypeStruct((1,...  8.01 us

profile of v2, /device:TPU:32, one launch (start us, length us, event | category | flops | bytes accessed | tf_op | source)
XLA Modules:
  0.0 113.7 jit_solution(9387742201235685447)
XLA Ops:
  0.0 0.0 copy-start
  0.0 1.0 copy-done
  1.0 0.0 copy-start.1
  1.0 0.7 copy-done.1
  1.7 104.1 %exchange.1.u_ref = bf16[2,512,2048]{2,1,0:T(8,128)(2,1)S(1)} custom-call(bf16[2,16,32,2048]{3,2,1,0:T(8,128)(2,1)} %v_ref.1, f32[16,64]{1,0:T(8,128)S(1)} %copy-done.1, f32[528,128]{1,0:T(8,128)S(1)} %copy-done), custom_call_target="tpu_custom_call" | custom-call | tf_op jit(solution)/shard_map/exchange/pallas_call | solution.py:421
  105.7 8.0 %gram.1 = bf16[1,8,2,512,512]{4,3,2,1,0:T(8,128)(2,1)} custom-call(bf16[2,512,2048]{2,1,0:T(8,128)(2,1)S(1)} %exchange.1.u_ref), custom_call_target="tpu_custom_call" | custom-call | tf_op jit(solution)/shard_map/gram/pallas_call | solution.py:453
Async XLA Ops:
  0.0 1.0 copy-start
  1.0 0.7 copy-start.1

commit v3 on v2

--- a/solution.py
+++ b/solution.py
@@ -3,7 +3,6 @@
 
 import jax
 import jax.numpy as jnp
-import numpy as np
 from jax import lax
 from jax.experimental import pallas as pl
 from jax.experimental.pallas import tpu as pltpu
@@ -29,20 +28,9 @@
 NT_DIMS = (((1,), (1,)), ((), ()))
 
 
-def trig_rows():
-    b = np.arange(128) % CH
-    rows = []
-    for k in range(34):
-        rows.append(np.cos(2 * np.pi * ((k * b) % CH) / CH))
-    for k in range(32):
-        rows.append(np.sin(2 * np.pi * ((k * b) % CH) / CH))
-    table = np.stack(rows) / math.sqrt(CH)
-    return np.repeat(table, 8, axis=0).astype(np.float32)
-
-
 def comm_kernel(
-    v_ref, taps_hbm, trig_hbm, u_ref,
-    vbuf, taps_ref, trig_ref, sb, recv, jx, spec, xg, ub, zbuf,
+    v_ref, taps_hbm, u_ref,
+    vbuf, taps_ref, sb, recv, jx, spec, xg, ub, zbuf,
     w_hi, w_lo, ppad, t16, rc, rs,
     v_sem, c_sem, zs, zr, hs, hr, xs, xr, us,
 ):
@@ -66,17 +54,19 @@
         return 0
 
     def v_copy(i):
-        qt, h = i // 2, i % 2
+        qt, h = lax.div(i, 2), lax.rem(i, 2)
         return pltpu.make_async_copy(
-            v_ref.at[:, pl.ds(h * 8, 8), pl.ds(qt * 16, 16), :], vbuf.at[i], v_sem.at[i]
+            v_ref.at[:, pl.ds(pl.multiple_of(h * 8, 8), 8), pl.ds(pl.multiple_of(qt * 16, 16), 16), :],
+            vbuf.at[i],
+            v_sem.at[i],
         )
 
     taps_copy = pltpu.make_async_copy(taps_hbm, taps_ref, c_sem.at[0])
-    trig_copy = pltpu.make_async_copy(trig_hbm, trig_ref, c_sem.at[1])
-    for i in range(4):
+    first = lax.div(y, 2) * 2
+    pieces = (first, first + 1, 2 - first, 3 - first)
+    for i in pieces:
         v_copy(i).start()
     taps_copy.start()
-    trig_copy.start()
     lax.fori_loop(1, NY * NZ, greet_stn, 0)
     lax.fori_loop(1, NT, greet_tm, 0)
 
@@ -128,11 +118,13 @@
             device_id_type=MESH,
         )
 
-    def send_step(j):
+    def prepare(j):
         def put(lane, tile):
             sb[j, :, :, lane : lane + 512] = tile
 
         relayout(j, put)
+
+    def send_step(j):
         for dz in ORDER[:-1]:
             z_copy(j, dz).start()
 
@@ -298,15 +290,15 @@
 
         turn_pair(3, want, put)
 
-    for i in range(4):
-        v_copy(i).wait()
+    v_copy(pieces[0]).wait()
+    prepare(0)
     pl.semaphore_wait(barrier, NY * NZ - 1 + NT - 1)
-
-    def prime(j, _):
-        send_step(j)
-        return 0
-
-    lax.fori_loop(0, AHEAD, prime, 0)
+    send_step(0)
+    v_copy(pieces[1]).wait()
+    prepare(1)
+    send_step(1)
+    v_copy(pieces[2]).wait()
+    v_copy(pieces[3]).wait()
 
     def prime_late(j, _):
         def put(lane, tile):
@@ -319,7 +311,6 @@
     lax.fori_loop(FIRST, STEPS, prime_late, 0)
 
     taps_copy.wait()
-    trig_copy.wait()
     half = lax.broadcasted_iota(jnp.int32, (16, 128), 1) < CH
     taps = jnp.concatenate([taps_ref[...], taps_ref[...]], axis=1)
     ppad[...] = jnp.zeros_like(ppad)
@@ -331,7 +322,11 @@
 
     def weights(i, _):
         rows = pl.ds(pl.multiple_of(i * 16, 16), 16)
-        trig = trig_ref[rows, :]
+        sine = (i >= COS_ROWS // 16).astype(jnp.int32)
+        r = i * 16 + lax.broadcasted_iota(jnp.int32, (16, 128), 0) - sine * COS_ROWS
+        b = lax.broadcasted_iota(jnp.int32, (16, 128), 1)
+        turn = ((r >> 3) * b - sine * (CH // 4)) & (CH - 1)
+        trig = jnp.cos(turn.astype(F32) * (2 * math.pi / CH)) * (1 / math.sqrt(CH))
         for t in range(WIN // 128):
             lanes = slice(128 * t, 128 * t + 128)
             w = t16[:, lanes] * trig
@@ -349,6 +344,7 @@
         def _():
             @pl.when(j + AHEAD < FIRST)
             def _():
+                prepare(j + AHEAD)
                 send_step(j + AHEAD)
 
             @pl.when(j + AHEAD >= FIRST)
@@ -384,10 +380,6 @@
             part = sb.at[0]
             pltpu.make_async_copy(part, part, zs.at[j]).wait()
 
-        @pl.when(j >= FIRST)
-        def _():
-            wait_step(j)
-
         @pl.when(tm < NT - 1)
         def _():
             halo_copy(j).wait_send()
@@ -399,20 +391,50 @@
     lax.fori_loop(0, STEPS, finish, 0)
     for d in range(3):
         u_copy(d).wait()
+    for j in range(FIRST, STEPS):
+        wait_step(j)
 
 
 LATE_AT = 1
 
 
-def gram_kernel(u_ref, out_ref):
-    re, im = u_ref[0], u_ref[1]
-    u = jnp.concatenate([re, im], axis=1)
-    w = jnp.concatenate([im, -re], axis=1)
+def gram_kernel(u_ref, out_ref, held, sem):
+    half = 256
     scale = 1.0 / 256
-    real = lax.dot_general(u, u, NT_DIMS, preferred_element_type=F32)
-    out_ref[0, 0, 0] = (real * scale).astype(BF16)
-    imag = lax.dot_general(w, u, NT_DIMS, preferred_element_type=F32)
-    out_ref[0, 0, 1] = (imag * scale).astype(BF16)
+
+    def product(left, right):
+        g = lax.dot_general(left, right, NT_DIMS, preferred_element_type=F32)
+        return (g * scale).astype(BF16)
+
+    copies = []
+
+    def send(k, part, rows):
+        c = pltpu.make_async_copy(
+            held.at[k, part, rows], out_ref.at[0, k, part, rows], sem.at[len(copies)]
+        )
+        c.start()
+        copies.append(c)
+
+    top, bottom = pl.ds(0, half), pl.ds(half, half)
+    for k in range(8):
+        lanes = slice(256 * k, 256 * k + 256)
+        re, im = u_ref[0, :, lanes], u_ref[1, :, lanes]
+        u = jnp.concatenate([re, im], axis=1)
+        w = jnp.concatenate([im, -re], axis=1)
+        g = product(jnp.concatenate([u[:half], w[:half]], axis=0), u)
+        held[k, 0, top] = g[:half]
+        held[k, 1, top] = g[half:]
+        send(k, 0, top)
+        send(k, 1, top)
+        held[k, 0, bottom, :half] = g[:half, half:].T
+        held[k, 1, bottom, :half] = -(g[half:, half:].T)
+        g = product(jnp.concatenate([u[half:], w[half:]], axis=0), u[half:])
+        held[k, 0, bottom, half:] = g[:half]
+        held[k, 1, bottom, half:] = g[half:]
+        send(k, 0, bottom)
+        send(k, 1, bottom)
+    for c in copies:
+        c.wait()
 
 
 def body(voltages, fir_taps):
@@ -421,12 +443,11 @@
     gathered = pl.pallas_call(
         comm_kernel,
         out_shape=jax.ShapeDtypeStruct((2, 512, 8 * 256), BF16),
-        in_specs=[pl.BlockSpec(memory_space=pltpu.HBM)] * 3,
+        in_specs=[pl.BlockSpec(memory_space=pltpu.HBM)] * 2,
         out_specs=any_space,
         scratch_shapes=[
             pltpu.VMEM((4, 2, 8, 16, N), BF16),
             pltpu.VMEM((16, CH), F32),
-            pltpu.VMEM((COS_ROWS + SIN_ROWS, 128), F32),
             pltpu.VMEM((FIRST, NZ, ROWS, N), BF16),
             pltpu.VMEM((STEPS, NZ, ROWS, HIST + N), BF16),
             pltpu.VMEM((LANES, HIST + N), BF16),
@@ -441,7 +462,7 @@
             pltpu.VMEM((COS_ROWS, 256), F32),
             pltpu.VMEM((SIN_ROWS, 256), F32),
             dma((4,)),
-            dma((2,)),
+            dma((1,)),
         ]
         + [dma((STEPS,))] * 6
         + [dma((3,))],
@@ -449,14 +470,14 @@
             collective_id=0, has_side_effects=True, vmem_limit_bytes=48 * 2**20
         ),
         name="exchange",
-    )(voltages, fir_taps, jnp.asarray(trig_rows()))
+    )(voltages, fir_taps)
     return pl.pallas_call(
         gram_kernel,
-        grid=(8,),
         out_shape=jax.ShapeDtypeStruct((1, 8, 2, 512, 512), BF16),
-        in_specs=[pl.BlockSpec((2, 512, 256), lambda k: (0, 0, k))],
-        out_specs=pl.BlockSpec((1, 1, 2, 512, 512), lambda k: (0, k, 0, 0, 0)),
-        compiler_params=pltpu.CompilerParams(vmem_limit_bytes=16 * 2**20),
+        in_specs=[pl.BlockSpec(memory_space=pltpu.VMEM)],
+        out_specs=any_space,
+        scratch_shapes=[pltpu.VMEM((8, 2, 512, 512), BF16), dma((32,))],
+        compiler_params=pltpu.CompilerParams(vmem_limit_bytes=24 * 2**20),
         name="gram",
     )(gathered)
 

time: 114 us -> 110 us (0.965)
  Pallas kernels: 112 us -> 108 us
    pallas_call x1, Pallas kernels: 8.01 us -> 4.83 us  [body(): pl.pallas_call(gram_kernel, out_shape=jax.ShapeDtypeStruct((1, 8, 2, 512,...]
where the time goes in v3:
time: 110 us; the launch traced here: 109 us
  Pallas kernels  108 us (98%)
    pallas_call x1, Pallas kernels, body(): pl.pallas_call(comm_kernel, out_shape=jax.ShapeDtypeStruct((2, 512, 8 * 2...  104 us
    pallas_call x1, Pallas kernels, body(): pl.pallas_call(gram_kernel, out_shape=jax.ShapeDtypeStruct((1, 8, 2, 512,...  4.83 us

profile of v3, /device:TPU:32, one launch (start us, length us, event | category | flops | bytes accessed | tf_op | source)
XLA Modules:
  0.0 109.1 jit_solution(10441298967666752236)
XLA Ops:
  0.0 0.0 copy-start
  0.0 0.7 copy-done
  0.7 103.6 %exchange.1.u_ref = bf16[2,512,2048]{2,1,0:T(8,128)(2,1)S(1)} custom-call(bf16[2,16,32,2048]{3,2,1,0:T(8,128)(2,1)} %v_ref.1, f32[16,64]{1,0:T(8,128)S(1)} %copy-done), custom_call_target="tpu_custom_call" | custom-call | tf_op jit(solution)/shard_map/exchange/pallas_call | solution.py:443
  104.3 4.8 %gram.1 = bf16[1,8,2,512,512]{4,3,2,1,0:T(8,128)(2,1)} custom-call(bf16[2,512,2048]{2,1,0:T(8,128)(2,1)S(1)} %exchange.1.u_ref), custom_call_target="tpu_custom_call" | custom-call | tf_op jit(solution)/shard_map/gram/pallas_call | solution.py:474
Async XLA Ops:
  0.0 0.7 copy-start

commit v4 on v3

--- a/solution.py
+++ b/solution.py
@@ -32,7 +32,7 @@
     v_ref, taps_hbm, u_ref,
     vbuf, taps_ref, sb, recv, jx, spec, xg, ub, zbuf,
     w_hi, w_lo, ppad, t16, rc, rs,
-    v_sem, c_sem, zs, zr, hs, hr, xs, xr, us,
+    round_sem, v_sem, c_sem, zs, zr, hs, hr, xs, xr, us,
 ):
     stn = lax.axis_index("stn")
     tm = lax.axis_index("tm")
@@ -41,17 +41,12 @@
 
     barrier = pltpu.get_barrier_semaphore()
 
-    def greet_stn(i, _):
-        pl.semaphore_signal(
-            barrier, inc=1, device_id=(lax.rem(stn + i, NY * NZ), tm), device_id_type=MESH
-        )
-        return 0
-
-    def greet_tm(i, _):
-        pl.semaphore_signal(
-            barrier, inc=1, device_id=(stn, lax.rem(tm + i, NT)), device_id_type=MESH
-        )
-        return 0
+    in_row = [(y * NZ + lax.rem(z + i, NZ), tm) for i in range(1, NZ)]
+    in_column = [(lax.rem(y + i, NY) * NZ + z, tm) for i in range(1, NY)]
+    sibling = [(stn, tm + 1 - 2 * lax.rem(tm, 2))]
+    in_line = [(stn, lax.rem(tm + 2 * i, NT)) for i in range(1, NT // 2)]
+    greeted = in_row + in_column + sibling + in_line
+    crossed = in_column + in_line
 
     def v_copy(i):
         qt, h = lax.div(i, 2), lax.rem(i, 2)
@@ -64,11 +59,11 @@
     taps_copy = pltpu.make_async_copy(taps_hbm, taps_ref, c_sem.at[0])
     first = lax.div(y, 2) * 2
     pieces = (first, first + 1, 2 - first, 3 - first)
+    for device in greeted:
+        pl.semaphore_signal(barrier, inc=1, device_id=device, device_id_type=MESH)
     for i in pieces:
         v_copy(i).start()
     taps_copy.start()
-    lax.fori_loop(1, NY * NZ, greet_stn, 0)
-    lax.fori_loop(1, NT, greet_tm, 0)
 
     def relayout(j, put):
         d, h = lax.div(j, 2), lax.rem(j, 2)
@@ -292,11 +287,14 @@
 
     v_copy(pieces[0]).wait()
     prepare(0)
-    pl.semaphore_wait(barrier, NY * NZ - 1 + NT - 1)
+    pl.semaphore_wait(barrier, len(greeted))
     send_step(0)
+    for device in crossed:
+        pl.semaphore_signal(round_sem, inc=1, device_id=device, device_id_type=MESH)
     v_copy(pieces[1]).wait()
     prepare(1)
     send_step(1)
+    pl.semaphore_wait(round_sem, len(crossed))
     v_copy(pieces[2]).wait()
     v_copy(pieces[3]).wait()
 
@@ -461,6 +459,7 @@
             pltpu.VMEM((16, WIN), F32),
             pltpu.VMEM((COS_ROWS, 256), F32),
             pltpu.VMEM((SIN_ROWS, 256), F32),
+            pltpu.SemaphoreType.REGULAR,
             dma((4,)),
             dma((1,)),
         ]

time: 110 us -> 107 us (0.973)
  Pallas kernels: 108 us -> 106 us
    pallas_call x1, Pallas kernels: 104 us -> 101 us  [body(): pl.pallas_call(comm_kernel, out_shape=jax.ShapeDtypeStruct((2, 512, 8 * 2...]
where the time goes in v4:
time: 107 us
  Pallas kernels  106 us (99%)
    pallas_call x1, Pallas kernels, body(): pl.pallas_call(comm_kernel, out_shape=jax.ShapeDtypeStruct((2, 512, 8 * 2...  101 us
    pallas_call x1, Pallas kernels, body(): pl.pallas_call(gram_kernel, out_shape=jax.ShapeDtypeStruct((1, 8, 2, 512,...  4.83 us

profile of v4, /device:TPU:32, one launch (start us, length us, event | category | flops | bytes accessed | tf_op | source)
XLA Modules:
  0.0 106.7 jit_solution(10344550406763686596)
XLA Ops:
  0.0 0.0 copy-start
  0.0 0.7 copy-done
  0.7 101.1 %exchange.1.u_ref = bf16[2,512,2048]{2,1,0:T(8,128)(2,1)S(1)} custom-call(bf16[2,16,32,2048]{3,2,1,0:T(8,128)(2,1)} %v_ref.1, f32[16,64]{1,0:T(8,128)S(1)} %copy-done), custom_call_target="tpu_custom_call" | custom-call | tf_op jit(solution)/shard_map/exchange/pallas_call | solution.py:441
  101.8 4.8 %gram.1 = bf16[1,8,2,512,512]{4,3,2,1,0:T(8,128)(2,1)} custom-call(bf16[2,512,2048]{2,1,0:T(8,128)(2,1)S(1)} %exchange.1.u_ref), custom_call_target="tpu_custom_call" | custom-call | tf_op jit(solution)/shard_map/gram/pallas_call | solution.py:473
Async XLA Ops:
  0.0 0.7 copy-start

commit v5 on v4

--- a/solution.py
+++ b/solution.py
@@ -29,10 +29,10 @@
 
 
 def comm_kernel(
-    v_ref, taps_hbm, u_ref,
-    vbuf, taps_ref, sb, recv, jx, spec, xg, ub, zbuf,
+    v_ref, taps_hbm, u_ref, g_ref,
+    vbuf, taps_ref, sb, recv, jx, spec, xg, ua, ub, zbuf, gbuf,
     w_hi, w_lo, ppad, t16, rc, rs,
-    round_sem, v_sem, c_sem, zs, zr, hs, hr, xs, xr, us,
+    round_sem, v_sem, c_sem, zs, zr, hs, hr, xs, xr, us, gs,
 ):
     stn = lax.axis_index("stn")
     tm = lax.axis_index("tm")
@@ -102,11 +102,11 @@
 
     def late_copy(j, dz):
         zt, to = z_target(j, dz)
-        ri = lax.rem(j, 2)
+        target = ua if j == FIRST else u_ref
         at = pl.multiple_of(y * 128 + z * 16, 16)
         return pltpu.make_async_remote_copy(
-            src_ref=zbuf.at[zt, ri],
-            dst_ref=u_ref.at[ri, pl.ds(at, 16), :],
+            src_ref=zbuf.at[zt, j - FIRST],
+            dst_ref=target.at[:, pl.ds(at, 16), :],
             send_sem=zs.at[j],
             recv_sem=zr.at[j],
             device_id=to,
@@ -242,13 +242,13 @@
     def wait_spectra(j):
         pltpu.make_async_copy(spec.at[j], spec.at[j], xr.at[j]).wait()
 
-    def turn_pair(d, want, put):
+    def turn_pair(d, want, put, put_rest):
         wait_spectra(2 * d)
         wait_spectra(2 * d + 1)
         c = lax.broadcasted_iota(jnp.int32, (256, 256), 1)
         perm = jnp.where(c == want, 1.0, 0.0).astype(BF16)
 
-        def channel(k, _):
+        def channel(k, store):
             a = jnp.concatenate(
                 [
                     xg[2 * d, :, :, k].reshape(256, LANES),
@@ -257,23 +257,37 @@
                 axis=1,
             )
             t = lax.dot_general(perm, a, NT_DIMS, preferred_element_type=F32)
-            put(pl.ds(pl.multiple_of(k * 256, 256), 256), t.astype(BF16))
+            lanes = pl.ds(pl.multiple_of((k % 4) * 256, 256), 256)
+            store(lanes, t.astype(BF16))
+
+        def early(k, _):
+            channel(k, put)
             return 0
 
-        lax.fori_loop(0, 8, channel, 0)
+        def rest(k, _):
+            channel(k, put_rest)
+            return 0
+
+        lax.fori_loop(0, 4, early, 0)
+        lax.fori_loop(4, 8, rest, 0)
+
+    def rows_of(d):
+        return pl.ds(pl.multiple_of(lax.rem(y + NY - d, NY) * 128, 128), 128)
 
     def u_copy(d):
-        at = pl.multiple_of(lax.rem(y + NY - d, NY) * 128, 128)
-        return pltpu.make_async_copy(ub.at[d], u_ref.at[:, pl.ds(at, 128), :], us.at[d])
+        return pltpu.make_async_copy(ub.at[d], u_ref.at[:, rows_of(d), :], us.at[d])
 
     def turn_early(d):
         o = lax.broadcasted_iota(jnp.int32, (256, 256), 0)
         want = ((o >> 3) & 1) * 128 + ((o >> 4) & 7) * 16 + (o >> 7) * 8 + (o & 7)
 
         def put(lanes, t):
+            ua[:, rows_of(d), lanes] = t.reshape(2, 128, 256)
+
+        def put_rest(lanes, t):
             ub[d, :, :, lanes] = t.reshape(2, 128, 256)
 
-        turn_pair(d, want, put)
+        turn_pair(d, want, put, put_rest)
         u_copy(d).start()
 
     def turn_late():
@@ -281,9 +295,12 @@
         want = ((o >> 3) & 1) * 128 + (o >> 5) * 16 + ((o >> 4) & 1) * 8 + (o & 7)
 
         def put(lanes, t):
-            zbuf[:, :, :, lanes] = t.reshape(NZ, 2, 16, 256)
-
-        turn_pair(3, want, put)
+            zbuf[:, 0, :, :, lanes] = t.reshape(NZ, 2, 16, 256)
+
+        def put_rest(lanes, t):
+            zbuf[:, 1, :, :, lanes] = t.reshape(NZ, 2, 16, 256)
+
+        turn_pair(3, want, put, put_rest)
 
     v_copy(pieces[0]).wait()
     prepare(0)
@@ -345,9 +362,10 @@
                 prepare(j + AHEAD)
                 send_step(j + AHEAD)
 
-            @pl.when(j + AHEAD >= FIRST)
-            def _():
-                send_late(j + AHEAD)
+            for late in range(FIRST, STEPS):
+                @pl.when(j + AHEAD == late)
+                def _(late=late):
+                    send_late(late)
 
             wait_step(j)
             send_halo(j)
@@ -366,6 +384,19 @@
 
     lax.fori_loop(0, STEPS, step, 0)
     turn_early(2)
+
+    def g_copy(k):
+        return pltpu.make_async_copy(gbuf.at[k], g_ref.at[k], gs.at[k])
+
+    wait_step(FIRST)
+
+    def make_gram(k, _):
+        lanes = pl.ds(pl.multiple_of(k * 256, 256), 256)
+        gram_into(gbuf.at[k], ua[0, :, lanes], ua[1, :, lanes])
+        g_copy(k).start()
+        return 0
+
+    lax.fori_loop(0, 4, make_gram, 0)
 
     def finish(j, _):
         @pl.when(j < 2)
@@ -389,48 +420,57 @@
     lax.fori_loop(0, STEPS, finish, 0)
     for d in range(3):
         u_copy(d).wait()
-    for j in range(FIRST, STEPS):
-        wait_step(j)
+    for k in range(4):
+        g_copy(k).wait()
+    wait_step(STEPS - 1)
 
 
 LATE_AT = 1
 
 
-def gram_kernel(u_ref, out_ref, held, sem):
+def gram_into(to, re, im, sent=lambda part, rows: None):
     half = 256
-    scale = 1.0 / 256
+    top, bottom = slice(0, half), slice(half, 2 * half)
 
     def product(left, right):
         g = lax.dot_general(left, right, NT_DIMS, preferred_element_type=F32)
-        return (g * scale).astype(BF16)
-
-    copies = []
-
-    def send(k, part, rows):
-        c = pltpu.make_async_copy(
-            held.at[k, part, rows], out_ref.at[0, k, part, rows], sem.at[len(copies)]
-        )
+        return (g * (1.0 / 256)).astype(BF16)
+
+    u = jnp.concatenate([re, im], axis=1)
+    w = jnp.concatenate([im, -re], axis=1)
+    g = product(jnp.concatenate([u[top], w[top]], axis=0), u)
+    to[0, top, :] = g[top]
+    to[1, top, :] = g[bottom]
+    sent(0, pl.ds(0, half))
+    sent(1, pl.ds(0, half))
+    to[0, bottom, top] = g[top, bottom].T
+    to[1, bottom, top] = -(g[bottom, bottom].T)
+    g = product(jnp.concatenate([u[bottom], w[bottom]], axis=0), u[bottom])
+    to[0, bottom, bottom] = g[top]
+    to[1, bottom, bottom] = g[bottom]
+    sent(0, pl.ds(half, half))
+    sent(1, pl.ds(half, half))
+
+
+def gram_kernel(u_ref, g_ref, out_ref, held, g_sem, sem):
+    copies = [
+        pltpu.make_async_copy(g_ref.at[k], out_ref.at[0, k], g_sem.at[k]) for k in range(4)
+    ]
+    for c in copies:
         c.start()
-        copies.append(c)
-
-    top, bottom = pl.ds(0, half), pl.ds(half, half)
-    for k in range(8):
+    for k in range(4):
         lanes = slice(256 * k, 256 * k + 256)
-        re, im = u_ref[0, :, lanes], u_ref[1, :, lanes]
-        u = jnp.concatenate([re, im], axis=1)
-        w = jnp.concatenate([im, -re], axis=1)
-        g = product(jnp.concatenate([u[:half], w[:half]], axis=0), u)
-        held[k, 0, top] = g[:half]
-        held[k, 1, top] = g[half:]
-        send(k, 0, top)
-        send(k, 1, top)
-        held[k, 0, bottom, :half] = g[:half, half:].T
-        held[k, 1, bottom, :half] = -(g[half:, half:].T)
-        g = product(jnp.concatenate([u[half:], w[half:]], axis=0), u[half:])
-        held[k, 0, bottom, half:] = g[:half]
-        held[k, 1, bottom, half:] = g[half:]
-        send(k, 0, bottom)
-        send(k, 1, bottom)
+
+        def sent(part, rows, k=k):
+            c = pltpu.make_async_copy(
+                held.at[k, part, rows],
+                out_ref.at[0, k + 4, part, rows],
+                sem.at[len(copies) - 4],
+            )
+            c.start()
+            copies.append(c)
+
+        gram_into(held.at[k], u_ref[0, :, lanes], u_ref[1, :, lanes], sent)
     for c in copies:
         c.wait()
 
@@ -438,11 +478,14 @@
 def body(voltages, fir_taps):
     dma = pltpu.SemaphoreType.DMA
     any_space = pl.BlockSpec(memory_space=pl.ANY)
-    gathered = pl.pallas_call(
+    u, g = pl.pallas_call(
         comm_kernel,
-        out_shape=jax.ShapeDtypeStruct((2, 512, 8 * 256), BF16),
+        out_shape=[
+            jax.ShapeDtypeStruct((2, 512, 4 * 256), BF16),
+            jax.ShapeDtypeStruct((4, 2, 512, 512), BF16),
+        ],
         in_specs=[pl.BlockSpec(memory_space=pltpu.HBM)] * 2,
-        out_specs=any_space,
+        out_specs=[any_space, any_space],
         scratch_shapes=[
             pltpu.VMEM((4, 2, 8, 16, N), BF16),
             pltpu.VMEM((16, CH), F32),
@@ -451,8 +494,10 @@
             pltpu.VMEM((LANES, HIST + N), BF16),
             pltpu.VMEM((STEPS, 2, CH, 16, 128), BF16),
             pltpu.VMEM((STEPS, NT, 2, 8, 16, 128), BF16),
-            pltpu.VMEM((3, 2, 128, 8 * 256), BF16),
-            pltpu.VMEM((NZ, 2, 16, 8 * 256), BF16),
+            pltpu.VMEM((2, 512, 4 * 256), BF16),
+            pltpu.VMEM((3, 2, 128, 4 * 256), BF16),
+            pltpu.VMEM((NZ, 2, 2, 16, 4 * 256), BF16),
+            pltpu.VMEM((4, 2, 512, 512), BF16),
             pltpu.VMEM((COS_ROWS + SIN_ROWS, WIN), BF16),
             pltpu.VMEM((COS_ROWS + SIN_ROWS, WIN), BF16),
             pltpu.VMEM((32, 128), F32),
@@ -464,21 +509,21 @@
             dma((1,)),
         ]
         + [dma((STEPS,))] * 6
-        + [dma((3,))],
+        + [dma((3,)), dma((4,))],
         compiler_params=pltpu.CompilerParams(
-            collective_id=0, has_side_effects=True, vmem_limit_bytes=48 * 2**20
+            collective_id=0, has_side_effects=True, vmem_limit_bytes=44 * 2**20
         ),
         name="exchange",
     )(voltages, fir_taps)
     return pl.pallas_call(
         gram_kernel,
         out_shape=jax.ShapeDtypeStruct((1, 8, 2, 512, 512), BF16),
-        in_specs=[pl.BlockSpec(memory_space=pltpu.VMEM)],
+        in_specs=[pl.BlockSpec(memory_space=pltpu.VMEM), any_space],
         out_specs=any_space,
-        scratch_shapes=[pltpu.VMEM((8, 2, 512, 512), BF16), dma((32,))],
+        scratch_shapes=[pltpu.VMEM((4, 2, 512, 512), BF16), dma((4,)), dma((16,))],
         compiler_params=pltpu.CompilerParams(vmem_limit_bytes=24 * 2**20),
         name="gram",
-    )(gathered)
+    )(u, g)
 
 
 def solution(mesh):

time: 107 us -> 105 us (0.981)
    pallas_call x1, Pallas kernels: 4.83 us -> 3.44 us  [body(): pl.pallas_call(gram_kernel, out_shape=jax.ShapeDtypeStruct((1, 8, 2, 512,...]
where the time goes in v5:
time: 105 us
  Pallas kernels  105 us (100%)
    pallas_call x1, Pallas kernels, body(): pl.pallas_call(comm_kernel, out_shape=[jax.ShapeDtypeStruct((2, 512, 4 *...  101 us
    pallas_call x1, Pallas kernels, body(): pl.pallas_call(gram_kernel, out_shape=jax.ShapeDtypeStruct((1, 8, 2, 512,...  3.44 us

profile of v5, /device:TPU:32, one launch (start us, length us, event | category | flops | bytes accessed | tf_op | source)
XLA Modules:
  0.0 105.3 jit_solution(6512457071166735502)
XLA Ops:
  0.0 0.0 copy-start
  0.0 0.7 copy-done
  0.7 101.2 %exchange.1 = (bf16[2,512,1024]{2,1,0:T(8,128)(2,1)S(1)}, bf16[4,2,512,512]{3,2,1,0:T(8,128)(2,1)S(1)}) custom-call(bf16[2,16,32,2048]{3,2,1,0:T(8,128)(2,1)} %v_ref.1, f32[16,64]{1,0:T(8,128)S(1)} %copy-done), custom_call_target="tpu_custom_call" | custom-call | tf_op jit(solution)/shard_map/exchange/pallas_call | solution.py:481
  101.9 3.4 %gram.1 = bf16[1,8,2,512,512]{4,3,2,1,0:T(8,128)(2,1)} custom-call(bf16[2,512,1024]{2,1,0:T(8,128)(2,1)S(1)} %get-tuple-element.7.u_ref, bf16[4,2,512,512]{3,2,1,0:T(8,128)(2,1)S(1)} %get-tuple-element.8.g_ref), custom_call_target="tpu_custom_call" | custom-call | tf_op jit(solution)/shard_map/gram/pallas_call | solution.py:518
Async XLA Ops:
  0.0 0.7 copy-start

commit v6 on v5

--- a/solution.py
+++ b/solution.py
@@ -59,9 +59,10 @@
     taps_copy = pltpu.make_async_copy(taps_hbm, taps_ref, c_sem.at[0])
     first = lax.div(y, 2) * 2
     pieces = (first, first + 1, 2 - first, 3 - first)
+    v_copy(pieces[0]).start()
     for device in greeted:
         pl.semaphore_signal(barrier, inc=1, device_id=device, device_id_type=MESH)
-    for i in pieces:
+    for i in pieces[1:]:
         v_copy(i).start()
     taps_copy.start()
 

time: 105 us -> 105 us (level)
  no operation moved by 1% of the time
where the time goes in v6:
time: 105 us
  Pallas kernels  105 us (100%)
    pallas_call x1, Pallas kernels, body(): pl.pallas_call(comm_kernel, out_shape=[jax.ShapeDtypeStruct((2, 512, 4 *...  101 us
    pallas_call x1, Pallas kernels, body(): pl.pallas_call(gram_kernel, out_shape=jax.ShapeDtypeStruct((1, 8, 2, 512,...  3.44 us

profile of v6, /device:TPU:32, one launch (start us, length us, event | category | flops | bytes accessed | tf_op | source)
XLA Modules:
  0.0 105.3 jit_solution(4561835541900203406)
XLA Ops:
  0.0 0.0 copy-start
  0.0 0.7 copy-done
  0.7 101.2 %exchange.1 = (bf16[2,512,1024]{2,1,0:T(8,128)(2,1)S(1)}, bf16[4,2,512,512]{3,2,1,0:T(8,128)(2,1)S(1)}) custom-call(bf16[2,16,32,2048]{3,2,1,0:T(8,128)(2,1)} %v_ref.1, f32[16,64]{1,0:T(8,128)S(1)} %copy-done), custom_call_target="tpu_custom_call" | custom-call | tf_op jit(solution)/shard_map/exchange/pallas_call | solution.py:482
  101.9 3.4 %gram.1 = bf16[1,8,2,512,512]{4,3,2,1,0:T(8,128)(2,1)} custom-call(bf16[2,512,1024]{2,1,0:T(8,128)(2,1)S(1)} %get-tuple-element.7.u_ref, bf16[4,2,512,512]{3,2,1,0:T(8,128)(2,1)S(1)} %get-tuple-element.8.g_ref), custom_call_target="tpu_custom_call" | custom-call | tf_op jit(solution)/shard_map/gram/pallas_call | solution.py:519
Async XLA Ops:
  0.0 0.7 copy-start
